TPU v7x, 256 devices: a whole 4x4x8 slice. The times are simulated.
256 devices in a mesh: dp: 2 (over y_hi), fsdp: 8 (over x, y_lo), expert: 16 (over z, core).
Axes of the slice: x: 4, y: 4 (y_hi: 2, y_lo: 2; y = y_hi * 2 + y_lo), z: 8, core: 2. Of those that a mesh axis runs over, the one named last changes fastest.
Arguments:
- tokens: bfloat16 [65536, 2048], P(('dp', 'fsdp', 'expert')), may hold values from -6 to 6
- expert_ids: int32 [65536, 8], P(('dp', 'fsdp', 'expert')), may hold values from 0 to 127, all different within a row; in each aligned block of 256 rows (0 to 255, 256 to 511, ...) at most 24 rows name the same one
- gate_units: int32 [65536, 8], P(('dp', 'fsdp', 'expert')), may hold values from 1 to 256
- expert_weights: bfloat16 [16, 2048, 3, 768], P('expert', ('dp', 'fsdp')), may hold values from -0.125 to 0.125
- out_grad: bfloat16 [65536, 2048], P(('dp', 'fsdp', 'expert')), may hold values from -6 to 6
Outputs:
- moe_out: bfloat16 [65536, 2048], P(('dp', 'fsdp', 'expert'))
- token_grad: bfloat16 [65536, 2048], P(('dp', 'fsdp', 'expert'))
- weight_grad: bfloat16 [16, 2048, 3, 768], P('expert', ('dp', 'fsdp'))
Inputs may be any that keep to these rules, and one draw needn't show every extreme that they name: `expert_ids`: each row names 8 different experts; the 256 rows of one device name one expert at most 24 times.
All inputs are finite; a program needn't handle non-finite values.
Results may differ from a plain program's by a relative error of at most 0.018.
Values may be sent and summed in bfloat16 or wider, within the bound.
A program may use at most 128 MiB of HBM per device.

v0:
```python
import jax
import jax.numpy as jnp
from jax import lax
from jax.sharding import PartitionSpec as P

CAP = 24


def route_tables(expert_ids, gate_units, expert_count, capacity):
    tok_count, top_count = expert_ids.shape
    slot_count = expert_count * capacity
    flat_ids = expert_ids.reshape(tok_count * top_count)
    chosen = (flat_ids[:, None] == jnp.arange(expert_count, dtype=jnp.int32)[None, :]).astype(
        jnp.int32
    )
    before = jnp.cumsum(chosen, axis=0) - chosen
    ranking = jnp.sum(before * chosen, axis=1)
    inside = flat_ids < expert_count
    slot_of = jnp.where(inside, flat_ids * capacity + ranking, slot_count).reshape(
        tok_count, top_count
    )
    matches = slot_of.T[:, None, :] == jnp.arange(slot_count, dtype=jnp.int32)[None, :, None]
    dispatch = jnp.sum(matches.astype(jnp.int32), axis=0).astype(jnp.bfloat16)
    gate_values = gate_units.astype(jnp.float32) / 256.0
    combine = jnp.sum(jnp.where(matches, gate_values.T[:, None, :], 0.0), axis=0)
    return (dispatch, combine)


def on_device(tokens, expert_ids, gate_units, expert_weights, out_grad):
    expert_count = lax.axis_size("expert")
    dispatch, combine = route_tables(expert_ids, gate_units, expert_count, CAP)
    slot_count = expert_count * CAP
    model_width = tokens.shape[1]
    hidden_units = expert_weights.shape[3]
    send_rows = (
        jnp.dot(dispatch, tokens, preferred_element_type=jnp.float32)
        .astype(jnp.bfloat16)
        .reshape(expert_count, CAP, model_width)
    )
    send_grad = (
        jnp.dot(dispatch, out_grad, preferred_element_type=jnp.float32)
        .astype(jnp.bfloat16)
        .reshape(expert_count, CAP, model_width)
    )
    slot_gate = jnp.sum(combine, axis=1).astype(jnp.bfloat16).reshape(expert_count, CAP)
    recv_rows, recv_grad, recv_gate = (
        lax.all_to_all(send_rows, "expert", split_axis=0, concat_axis=0, tiled=True),
        lax.all_to_all(send_grad, "expert", split_axis=0, concat_axis=0, tiled=True),
        lax.all_to_all(slot_gate, "expert", split_axis=0, concat_axis=0, tiled=True),
    )
    full_weights = lax.all_gather(expert_weights, ("dp", "fsdp"), axis=1, tiled=True)
    flat_weights = full_weights.reshape(model_width, 3 * hidden_units)
    slot_rows = recv_rows.reshape(slot_count, model_width)
    gate_up = jnp.dot(
        slot_rows, flat_weights[:, : 2 * hidden_units], preferred_element_type=jnp.float32
    )
    gate_act = gate_up[:, :hidden_units]
    up_act = gate_up[:, hidden_units:]
    sigmoid_gate = jax.nn.sigmoid(gate_act)
    swish_gate = gate_act * sigmoid_gate
    activation = (swish_gate * up_act).astype(jnp.bfloat16)
    down_rows = flat_weights[:, 2 * hidden_units :]
    result = lax.dot_general(
        activation, down_rows, (((1,), (1,)), ((), ())), preferred_element_type=jnp.float32
    ).astype(jnp.bfloat16)
    returned = lax.all_to_all(
        result.reshape(expert_count, CAP, model_width),
        "expert",
        split_axis=0,
        concat_axis=0,
        tiled=True,
    )
    moe_out = lax.dot_general(
        combine.astype(jnp.bfloat16),
        returned.reshape(slot_count, model_width),
        (((0,), (0,)), ((), ())),
        preferred_element_type=jnp.float32,
    ).astype(jnp.bfloat16)
    grad_rows = recv_grad.reshape(slot_count, model_width)
    scaled = (
        recv_gate.reshape(slot_count, 1).astype(jnp.float32) * grad_rows.astype(jnp.float32)
    ).astype(jnp.bfloat16)
    hidden_grad = jnp.dot(scaled, down_rows, preferred_element_type=jnp.float32)
    gate_grad = (
        hidden_grad * up_act * sigmoid_gate * (1.0 + gate_act * (1.0 - sigmoid_gate))
    ).astype(jnp.bfloat16)
    up_grad = (hidden_grad * swish_gate).astype(jnp.bfloat16)
    pair_grad = jnp.concatenate([gate_grad, up_grad], axis=1)
    row_grad = lax.dot_general(
        pair_grad,
        flat_weights[:, : 2 * hidden_units],
        (((1,), (1,)), ((), ())),
        preferred_element_type=jnp.float32,
    ).astype(jnp.bfloat16)
    back_grads = lax.all_to_all(
        row_grad.reshape(expert_count, CAP, model_width),
        "expert",
        split_axis=0,
        concat_axis=0,
        tiled=True,
    )
    token_grad = lax.dot_general(
        dispatch,
        back_grads.reshape(slot_count, model_width),
        (((0,), (0,)), ((), ())),
        preferred_element_type=jnp.float32,
    ).astype(jnp.bfloat16)
    input_term = lax.dot_general(
        slot_rows, pair_grad, (((0,), (0,)), ((), ())), preferred_element_type=jnp.float32
    )
    down_term = lax.dot_general(
        scaled, activation, (((0,), (0,)), ((), ())), preferred_element_type=jnp.float32
    )
    summed = lax.psum_scatter(
        jnp.concatenate([input_term, down_term], axis=1)
        .reshape(lax.axis_size(("dp", "fsdp")) * expert_weights.shape[1], 3, hidden_units)
        .astype(jnp.bfloat16),
        ("dp", "fsdp"),
        scatter_dimension=0,
        tiled=True,
    )
    weight_grad = summed.reshape(expert_weights.shape)
    return (moe_out, token_grad, weight_grad)


def solution(mesh):
    placed = (
        P(("dp", "fsdp", "expert"), None),
        P(("dp", "fsdp", "expert"), None),
        P(("dp", "fsdp", "expert"), None),
        P("expert", ("dp", "fsdp"), None, None),
        P(("dp", "fsdp", "expert"), None),
    )
    return jax.shard_map(
        on_device,
        mesh=mesh,
        in_specs=placed,
        out_specs=(
            P(("dp", "fsdp", "expert"), None),
            P(("dp", "fsdp", "expert"), None),
            P("expert", ("dp", "fsdp"), None, None),
        ),
        check_vma=False,
    )
```

profile of v0, /device:TPU:33, one launch (start us, length us, event | category | flops | bytes accessed | tf_op | source)
XLA Modules:
  0.0 470.5 jit_solution(17774609145026411051)
XLA Ops:
  7.2 0.0 copy-start
  7.2 0.0 all-gather.2.cloned.1.call-start
  7.2 2.2 copy.41
  9.4 0.0 all-gather.2.cloned.1.call-update
  9.5 0.8 copy.38
  10.3 0.1 eq.42
  10.4 0.1 eq.38
  10.5 4.5 reduce-window.6
  15.1 0.4 slice_reduce_fusion
  15.5 0.2 reduce-window.9
  15.7 0.1 broadcast_add_fusion
  15.8 0.1 fusion.15
  15.9 0.1 reduce_sum.39
  16.0 0.1 copy.40
  16.0 0.0 copy-done.3
  16.1 0.5 select_reduce_fusion
  16.5 0.7 convert_element_type.109
  17.2 8.9 %all-to-all-start.2 = ((bf16[16,1,24]{2,1,0:T(2,128)(2,1)}), bf16[16,1,24]{2,1,0:T(2,128)(2,1)S(1)}, u32[]{:S(2)}, u32[]{:S(2)}) async-start(bf16[16,1,24]{2,1,0:T(2,128)(2,1)} %convert_element_type.109), calls=%async_computation.2 | async-start | bytes 16384 | tf_op jit(solution)/shard_map/all_to_all | solution.py:49
  26.1 0.4 convert_reduce_fusion
  26.5 1.8 convolution_convert_fusion.3
  28.3 4.1 all-to-all-done.2
  32.4 4.9 %all-to-all-start.3 = ((bf16[16,24,2048]{2,1,0:T(8,128)(2,1)}), bf16[16,24,2048]{2,1,0:T(8,128)(2,1)S(1)}, u32[]{:S(2)}, u32[]{:S(2)}) async-start(bf16[16,24,2048]{2,1,0:T(8,128)(2,1)} %bitcast.8), calls=%async_computation.3 | async-start | bytes 3145728 | tf_op jit(solution)/shard_map/all_to_all | solution.py:48
  37.2 3.0 convolution_convert_fusion.4
  40.2 33.2 %all-to-all-done.3 = bf16[16,24,2048]{2,1,0:T(8,128)(2,1)S(1)} async-done(((bf16[16,24,2048]{2,1,0:T(8,128)(2,1)}), bf16[16,24,2048]{2,1,0:T(8,128)(2,1)S(1)}, u32[]{:S(2)}, u32[]{:S(2)}) %all-to-all-start.3) | async-done | bytes 1572896 | tf_op jit(solution)/shard_map/all_to_all | solution.py:48
  73.4 6.5 %all-to-all-start = ((bf16[16,24,2048]{2,1,0:T(8,128)(2,1)}), bf16[16,24,2048]{2,1,0:T(8,128)(2,1)}, u32[]{:S(2)}, u32[]{:S(2)}) async-start(bf16[16,24,2048]{2,1,0:T(8,128)(2,1)} %bitcast.3), calls=%async_computation | async-start | bytes 3145728 | tf_op jit(solution)/shard_map/all_to_all | solution.py:47
  80.0 0.2 reduce-scatter.2.cloned.1.call-start
  80.2 0.1 reshape.96
  80.3 1.5 fusion.4
  81.9 34.7 %all-to-all-done = bf16[16,24,2048]{2,1,0:T(8,128)(2,1)} async-done(((bf16[16,24,2048]{2,1,0:T(8,128)(2,1)}), bf16[16,24,2048]{2,1,0:T(8,128)(2,1)}, u32[]{:S(2)}, u32[]{:S(2)}) %all-to-all-start) | async-done | bytes 1572896 | tf_op jit(solution)/shard_map/all_to_all | solution.py:47
  116.5 99.4 %all-gather.2.cloned.1.call-done = bf16[1,2048,3,768]{1,3,2,0:T(8,128)(2,1)} async-done(((bf16[1,128,3,768]{1,3,2,0:T(8,128)(2,1)}), bf16[1,2048,3,768]{1,3,2,0:T(8,128)(2,1)}) %all-gather.2.cloned.1.call-update) | async-done | bytes 9437200 | tf_op jit(solution)/shard_map/all_gather | solution.py:51
  215.9 5.4 %fusion.2 = f32[384,1536]{1,0:T(8,128)S(1)} fusion(bf16[384,2048]{1,0:T(8,128)(2,1)} %bitcast.4, bf16[2048,2304]{0,1:T(8,128)(2,1)} %bitcast.53), kind=kOutput, calls=%fused_computation.4 | convolution fusion | flops 2415919104 | bytes 10223616 | tf_op jit(solution)/shard_map/dot_general | solution.py:54
  221.3 3.7 multiply_convert_fusion.1
  225.0 0.0 copy-start.5
  225.1 1.9 convolution_convert_fusion.1
  226.9 5.2 %convolution_convert_fusion = bf16[2048,1536]{0,1:T(8,128)(2,1)S(1)} fusion(bf16[384,2048]{1,0:T(8,128)(2,1)} %bitcast.4, bf16[384,768]{1,0:T(8,128)(2,1)S(1)} %get-tuple-element.6, bf16[384,768]{1,0:T(8,128)(2,1)S(1)} %get-tuple-element.5), kind=kOutput, calls=%fused_computation.1 | convolution fusion | flops 2421424128 | bytes 9043968 | tf_op jit(solution)/shard_map/dot_general | solution.py:108
  232.1 11.5 %pad_maximum_fusion = bf16[2048,2304]{0,1:T(8,128)(2,1)} fusion(bf16[2048,768]{0,1:T(8,128)(2,1)S(1)} %convolution_convert_fusion.1, bf16[2048,1536]{0,1:T(8,128)(2,1)S(1)} %convolution_convert_fusion), kind=kLoop, calls=%fused_computation | loop fusion | flops 18874368 | bytes 18874368 | tf_op jit(solution)/shard_map/concatenate | solution.py:115
  243.6 12.7 %copy.43 = bf16[2048,3,768]{2,0,1:T(8,128)(2,1)} copy(bf16[2048,3,768]{0,2,1:T(8,128)(2,1)} %bitcast.46) | data formatting | bytes 18874368 | tf_op jit(solution)/shard_map/convert_element_type | solution.py:117
  256.3 0.0 reduce-scatter.2.cloned.1.call-update
  256.4 4.5 convolution_convert_fusion.2
  260.8 9.0 %all-to-all-start.1 = ((bf16[16,24,2048]{2,1,0:T(8,128)(2,1)}), bf16[16,24,2048]{2,1,0:T(8,128)(2,1)S(1)}, u32[]{:S(2)}, u32[]{:S(2)}) async-start(bf16[16,24,2048]{2,1,0:T(8,128)(2,1)} %bitcast.50), calls=%async_computation.1 | async-start | bytes 3145728 | tf_op jit(solution)/shard_map/all_to_all | solution.py:66
  269.8 6.9 %fusion.5 = bf16[384,2048]{1,0:T(8,128)(2,1)} fusion(bf16[2048,2304]{0,1:T(8,128)(2,1)} %bitcast.56, bf16[384,768]{1,0:T(8,128)(2,1)} %copy-done.6, bf16[384,768]{1,0:T(8,128)(2,1)} %copy-done.5), kind=kOutput, calls=%fused_computation.14 | convolution fusion | flops 2419064832 | bytes 9043968 | tf_op jit(solution)/shard_map/dot_general | solution.py:89
  276.7 29.7 %all-to-all-done.1 = bf16[16,24,2048]{2,1,0:T(8,128)(2,1)S(1)} async-done(((bf16[16,24,2048]{2,1,0:T(8,128)(2,1)}), bf16[16,24,2048]{2,1,0:T(8,128)(2,1)S(1)}, u32[]{:S(2)}, u32[]{:S(2)}) %all-to-all-start.1) | async-done | bytes 1572896 | tf_op jit(solution)/shard_map/all_to_all | solution.py:66
  306.4 1.2 copy-done.1
  307.5 6.1 %all-to-all-start.4 = ((bf16[16,24,2048]{2,1,0:T(8,128)(2,1)}), bf16[16,24,2048]{2,1,0:T(8,128)(2,1)S(1)}, u32[]{:S(2)}, u32[]{:S(2)}) async-start(bf16[16,24,2048]{2,1,0:T(8,128)(2,1)} %bitcast.49), calls=%async_computation.4 | async-start | bytes 3145728 | tf_op jit(solution)/shard_map/all_to_all | solution.py:95
  313.6 3.1 convolution_convert_fusion.6
  316.7 33.5 %all-to-all-done.4 = bf16[16,24,2048]{2,1,0:T(8,128)(2,1)S(1)} async-done(((bf16[16,24,2048]{2,1,0:T(8,128)(2,1)}), bf16[16,24,2048]{2,1,0:T(8,128)(2,1)S(1)}, u32[]{:S(2)}, u32[]{:S(2)}) %all-to-all-start.4) | async-done | bytes 1572896 | tf_op jit(solution)/shard_map/all_to_all | solution.py:95
  350.2 1.7 convolution_convert_fusion.5
  351.9 111.8 %reduce-scatter.2.cloned.1.call-done = bf16[128,3,768]{2,0,1:T(8,128)(2,1)} async-done(((bf16[2048,3,768]{2,0,1:T(8,128)(2,1)}), bf16[128,3,768]{2,0,1:T(8,128)(2,1)}) %reduce-scatter.2.cloned.1.call-update) | async-done | bytes 589840 | tf_op jit(solution)/shard_map/reduce_scatter | solution.py:114
  (14 shorter events, 0.1 us)
Async XLA Ops:
  7.2 19.4 %copy-start = (bf16[256,2048]{1,0:T(8,128)(2,1)S(1)}, bf16[256,2048]{1,0:T(8,128)(2,1)}, u32[]{:S(2)}) copy-start(bf16[256,2048]{1,0:T(8,128)(2,1)} %param.9) | copy-start | bytes 3145732
  7.2 8.9 %copy-start.3 = (s32[256,8]{0,1:T(8,128)S(1)}, s32[256,8]{0,1:T(8,128)}, u32[]{:S(2)}) copy-start(s32[256,8]{0,1:T(8,128)} %param.6) | copy-start | bytes 24580
  7.2 8.8 %copy-start.4 = (s32[256,8]{0,1:T(8,128)S(1)}, s32[256,8]{0,1:T(8,128)}, u32[]{:S(2)}) copy-start(s32[256,8]{0,1:T(8,128)} %param.7) | copy-start | bytes 24580
  7.2 208.7 %all-gather.2.cloned.1.call-start = ((), (), s32[]{:S(2)}) async-start(), calls=%async_computation.6 | async-start | bytes 10027008 | tf_op jit(solution)/shard_map/all_gather | solution.py:51
  17.2 15.1 %all-to-all-start.2 = ((bf16[16,1,24]{2,1,0:T(2,128)(2,1)}), bf16[16,1,24]{2,1,0:T(2,128)(2,1)S(1)}, u32[]{:S(2)}, u32[]{:S(2)}) async-start(bf16[16,1,24]{2,1,0:T(2,128)(2,1)} %convert_element_type.109), calls=%async_computation.2 | async-start | bytes 16384 | tf_op jit(solution)/shard_map/all_to_all | solution.py:49
  32.4 41.1 %all-to-all-start.3 = ((bf16[16,24,2048]{2,1,0:T(8,128)(2,1)}), bf16[16,24,2048]{2,1,0:T(8,128)(2,1)S(1)}, u32[]{:S(2)}, u32[]{:S(2)}) async-start(bf16[16,24,2048]{2,1,0:T(8,128)(2,1)} %bitcast.8), calls=%async_computation.3 | async-start | bytes 3145728 | tf_op jit(solution)/shard_map/all_to_all | solution.py:48
  73.4 43.1 %all-to-all-start = ((bf16[16,24,2048]{2,1,0:T(8,128)(2,1)}), bf16[16,24,2048]{2,1,0:T(8,128)(2,1)}, u32[]{:S(2)}, u32[]{:S(2)}) async-start(bf16[16,24,2048]{2,1,0:T(8,128)(2,1)} %bitcast.3), calls=%async_computation | async-start | bytes 3145728 | tf_op jit(solution)/shard_map/all_to_all | solution.py:47
  80.0 383.7 %reduce-scatter.2.cloned.1.call-start = ((), (), s32[]{:S(2)}) async-start(), calls=%async_computation.7 | async-start | bytes 10027008 | tf_op jit(solution)/shard_map/reduce_scatter | solution.py:114
  215.9 5.4 %copy-start.2 = (bf16[384,2048]{1,0:T(8,128)(2,1)S(1)}, bf16[384,2048]{1,0:T(8,128)(2,1)}, u32[]{:S(2)}) copy-start(bf16[384,2048]{1,0:T(8,128)(2,1)} %fusion.4) | copy-start | bytes 4718596
  225.0 1.9 copy-start.5
  225.1 1.9 copy-start.6
  260.8 45.6 %all-to-all-start.1 = ((bf16[16,24,2048]{2,1,0:T(8,128)(2,1)}), bf16[16,24,2048]{2,1,0:T(8,128)(2,1)S(1)}, u32[]{:S(2)}, u32[]{:S(2)}) async-start(bf16[16,24,2048]{2,1,0:T(8,128)(2,1)} %bitcast.50), calls=%async_computation.1 | async-start | bytes 3145728 | tf_op jit(solution)/shard_map/all_to_all | solution.py:66
  306.4 1.2 copy-start.1
  307.5 42.7 %all-to-all-start.4 = ((bf16[16,24,2048]{2,1,0:T(8,128)(2,1)}), bf16[16,24,2048]{2,1,0:T(8,128)(2,1)S(1)}, u32[]{:S(2)}, u32[]{:S(2)}) async-start(bf16[16,24,2048]{2,1,0:T(8,128)(2,1)} %bitcast.49), calls=%async_computation.4 | async-start | bytes 3145728 | tf_op jit(solution)/shard_map/all_to_all | solution.py:95
Sparse Core Ops, SparseCore 0:
  10.3 205.5 all-gather.1
  256.5 207.1 reduce-scatter.1
where the time goes:
time: 474 us; the launch traced here: 471 us
  waiting for transfers between devices  346 us (73%)
  matrix products  37 us (8%)
  starting transfers between devices  35.6 us (8%)
  other arithmetic  18.8 us (4%)
  local copies, waits for them, and re-layouts  18.5 us (4%)
  between operations  14.2 us (3%)
    reduce_scatter x1, waiting for transfers between devices, on_device(): lax.psum_scatter(jnp.concatenate([input_term, down_term], axis=1).reshape...  112 us
    all_gather x1, waiting for transfers between devices, on_device(): lax.all_gather(expert_weights, ('dp', 'fsdp'), axis=1, tiled=True)  99.4 us
    all_to_all x1, waiting for transfers between devices, on_device(): lax.all_to_all(send_rows, 'expert', split_axis=0, concat_axis=0, tiled=True)  34.7 us
    all_to_all x1, waiting for transfers between devices, on_device(): lax.all_to_all(row_grad.reshape(expert_count, CAP, model_width), 'expert'...  33.5 us
    all_to_all x1, waiting for transfers between devices, on_device(): lax.all_to_all(send_grad, 'expert', split_axis=0, concat_axis=0, tiled=True)  33.2 us
    all_to_all x1, waiting for transfers between devices, on_device(): lax.all_to_all(result.reshape(expert_count, CAP, model_width), 'expert',...  29.7 us
    convert_element_type x1, local copies, waits for them, and re-layouts, on_device(): summed = lax.psum_scatter(jnp.concatenate([input_term, down_term], axis=1...  12.7 us
    concatenate x1, other arithmetic, on_device(): jnp.concatenate([input_term, down_term], axis=1)  11.5 us
  transfers between devices with their start and end apart: 7, of which 7 were waited for; matrix products, arithmetic and copies ran while one was open for 7% of the time, Pallas kernels for 0%

commit v1 on v0

v1 whole, which is shorter than its diff:
```python
import functools

import jax
import jax.numpy as jnp
from jax import lax
from jax.experimental import pallas as pl
from jax.experimental.pallas import tpu as pltpu
from jax.sharding import PartitionSpec as P

CAP = 24
SLOTS = 16
ROWS = CAP * SLOTS
MESH = pl.DeviceIdType.MESH
BF16 = jnp.bfloat16
F32 = jnp.float32

OFFSETS = [(dz, dc) for dz in (0, 1, 7, 2, 6, 3, 5, 4) for dc in (0, 1)]
CHUNKS = ((0, 10), (10, 14), (14, 16))
PIECES = ((0, 6), (6, 10), (10, 14), (14, 16))


def place():
    dp, fsdp, expert = (lax.axis_index(n) for n in ("dp", "fsdp", "expert"))
    return lax.div(fsdp, 2), dp * 2 + lax.rem(fsdp, 2), lax.div(expert, 2), lax.rem(expert, 2)


def device(x, y, z, core):
    return (lax.div(y, 2), x * 2 + lax.rem(y, 2), z * 2 + core)


def kernel(
    tokens, ids, units, weights, out_grad,
    moe_out, token_grad, weight_grad,
    full, term, reduced, row_send, grad_send, row_recv, grad_recv,
    res_send, back_send, res_recv, back_recv, rows, grads, act, gate_grad, up_grad,
    pick, weigh,
    out_s, out_r, ret_s, ret_r, ag_s, ag_r, rs_s, rs_r,
):
    x, y, z, core = place()
    width = tokens.shape[1]
    hidden = weights.shape[2]

    def peer(slot, sign):
        dz, dc = OFFSETS[slot]
        return device(x, y, lax.rem(z + (sign * dz) % 8, 8), lax.rem(core + dc, 2))

    def near(axis, step):
        if axis == 0:
            return device(lax.rem(x + step % 4, 4), y, z, core)
        return device(x, lax.rem(y + step % 4, 4), z, core)

    def block(half, first, second):
        dx, dy = (first, second) if half == 0 else (second, first)
        bx, by = lax.rem(x + dx % 4, 4), lax.rem(y + dy % 4, 4)
        return lax.div(by, 2) * 8 + bx * 2 + lax.rem(by, 2)

    barrier = pltpu.get_barrier_semaphore()
    for slot in range(1, SLOTS):
        pl.semaphore_signal(barrier, inc=1, device_id=peer(slot, 1), device_id_type=MESH)
    for axis in (0, 1):
        for step in (1, -1):
            pl.semaphore_signal(barrier, inc=1, device_id=near(axis, step), device_id_type=MESH)

    mine = block(0, 0, 0)
    full[mine] = weights[...]
    pl.semaphore_wait(barrier, SLOTS - 1 + 4)

    sent = []

    def send(src, dst, send_sem, recv_sem, to):
        copy = pltpu.make_async_remote_copy(
            src_ref=src, dst_ref=dst, send_sem=send_sem, recv_sem=recv_sem,
            device_id=to, device_id_type=MESH,
        )
        copy.start()
        sent.append(copy)
        return copy

    ag = {}

    def part(which, half):
        base = 64 * half
        return {"w": pl.ds(base, 64), "p": pl.ds(base, 32), "q": pl.ds(base + 32, 32)}[which]

    def gather_send(half, index, at, which, axis, step):
        ref = full.at[at, :, part(which, half), :]
        ag[half, index] = send(ref, ref, ag_s.at[half, index], ag_r.at[half, index], near(axis, step))

    ITEMS = (0, -1, 1, 2)

    def gather_own(half):
        a1, a2 = (0, 1) if half == 0 else (1, 0)
        gather_send(half, 0, mine, "w", a1, 1)
        gather_send(half, 1, mine, "w", a1, -1)

    def gather_item(half, k):
        a2 = 1 if half == 0 else 0
        at = block(half, ITEMS[k], 0)
        gather_send(half, 4 + 4 * k, at, "w", a2, 1)
        gather_send(half, 5 + 4 * k, at, "w", a2, -1)

    def gather_forward_first(half):
        a1 = 0 if half == 0 else 1
        ag[half, 0].wait_recv()
        gather_send(half, 2, block(half, -1, 0), "p", a1, 1)
        ag[half, 1].wait_recv()
        gather_send(half, 3, block(half, 1, 0), "q", a1, -1)

    def gather_forward_item(half, k):
        a2 = 1 if half == 0 else 0
        ag[half, 4 + 4 * k].wait_recv()
        gather_send(half, 6 + 4 * k, block(half, ITEMS[k], -1), "p", a2, 1)
        ag[half, 5 + 4 * k].wait_recv()
        gather_send(half, 7 + 4 * k, block(half, ITEMS[k], 1), "q", a2, -1)

    for half in (0, 1):
        gather_own(half)
    for half in (0, 1):
        gather_item(half, 0)

    lane = lax.broadcasted_iota(jnp.int32, (1, ROWS), 1)
    slot_of = jnp.zeros((1, ROWS), jnp.int32)
    for j in range(1, SLOTS):
        slot_of = slot_of + (lane >= CAP * j).astype(jnp.int32)
    rank_of = (lane - slot_of * CAP).astype(F32)
    pair = slot_of >> 1
    dz = jnp.where((pair & 1) == 1, (pair + 1) >> 1, (8 - (pair >> 1)) & 7)
    named = ((z + dz) & 7) * 2 + ((core + (slot_of & 1)) & 1)
    token_count = tokens.shape[0]
    chosen = jnp.zeros((token_count, ROWS), F32)
    id_table = ids[...]
    unit_table = units[...].astype(F32)
    for k in range(ids.shape[1]):
        chosen = chosen + jnp.where(id_table[:, k : k + 1] == named, unit_table[:, k : k + 1], 0.0)
    earlier = (
        lax.broadcasted_iota(jnp.int32, (token_count, token_count), 1)
        < lax.broadcasted_iota(jnp.int32, (token_count, token_count), 0)
    ).astype(F32).astype(BF16)
    ranking = jnp.dot(
        earlier, (chosen > 0.0).astype(F32).astype(BF16), preferred_element_type=F32
    )
    gate = jnp.where(ranking == rank_of, chosen, 0.0)
    weigh[...] = (jnp.transpose(gate) * (1.0 / 256.0)).astype(BF16)
    pick[...] = jnp.transpose((gate > 0.0).astype(F32)).astype(BF16)

    out = {}

    def dispatch(lo, hi):
        cols = 512

        def tile(i, _):
            at = pl.ds(pl.multiple_of(i * cols, cols), cols)
            for table, source, to in ((pick, tokens, row_send), (weigh, out_grad, grad_send)):
                got = jnp.dot(
                    table[CAP * lo : CAP * hi, :], source[:, at], preferred_element_type=F32
                )
                to[lo:hi, :, at] = got.reshape(hi - lo, CAP, cols).astype(BF16)
            return 0

        lax.fori_loop(0, width // cols, tile, 0)
        for slot in range(max(lo, 1), hi):
            for a, (src, dst) in enumerate(((row_send, row_recv), (grad_send, grad_recv))):
                out[a, slot] = send(
                    src.at[slot], dst.at[slot], out_s.at[a, slot], out_r.at[a, slot], peer(slot, 1)
                )

    dispatch(*PIECES[0])
    row_recv[0] = row_send[0]
    grad_recv[0] = grad_send[0]
    dispatch(*PIECES[1])
    for half in (0, 1):
        gather_forward_first(half)
    for half in (0, 1):
        gather_item(half, 1)
        gather_item(half, 2)
    dispatch(*PIECES[2])
    dispatch(*PIECES[3])
    for half in (0, 1):
        gather_forward_item(half, 0)
    for half in (0, 1):
        ag[half, 2].wait_recv()
        ag[half, 3].wait_recv()
        gather_item(half, 3)
    for k in (1, 2, 3):
        for half in (0, 1):
            gather_forward_item(half, k)
    for k in range(4):
        for half in (0, 1):
            ag[half, 6 + 4 * k].wait_recv()
            ag[half, 7 + 4 * k].wait_recv()

    ret = {}
    nt = (((1,), (1,)), ((), ()))
    tn = (((0,), (0,)), ((), ()))

    def experts(lo, hi):
        r0, r1 = CAP * lo, CAP * hi
        for slot in range(max(lo, 1), hi):
            for a in (0, 1):
                out[a, slot].wait_recv()

        def pack(i, _):
            at = pl.ds(pl.multiple_of(i * 512, 512), 512)
            for src, dst in ((row_recv, rows), (grad_recv, grads)):
                dst[r0:r1, at] = src[lo:hi, :, at].astype(F32).reshape(r1 - r0, 512).astype(BF16)
            return 0

        lax.fori_loop(0, width // 512, pack, 0)

        def inner(i, _):
            at = pl.ds(pl.multiple_of(i * 256, 256), 256)
            w = [full[:, j, :, at].reshape(width, 256) for j in range(3)]
            g = jnp.dot(rows[r0:r1, :], w[0], preferred_element_type=F32)
            u = jnp.dot(rows[r0:r1, :], w[1], preferred_element_type=F32)
            hg = jnp.dot(grads[r0:r1, :], w[2], preferred_element_type=F32)
            s = jax.nn.sigmoid(g)
            swish = g * s
            act[r0:r1, at] = (swish * u).astype(BF16)
            gate_grad[r0:r1, at] = (hg * u * s * (1.0 + g * (1.0 - s))).astype(BF16)
            up_grad[r0:r1, at] = (hg * swish).astype(BF16)
            return 0

        lax.fori_loop(0, hidden // 256, inner, 0)

        def outer(i, _):
            at = pl.ds(pl.multiple_of(i * 256, 256), 256)
            w = [full[pl.ds(2 * i, 2), j].reshape(256, hidden) for j in range(3)]
            res = lax.dot_general(act[r0:r1, :], w[2], nt, preferred_element_type=F32)
            res_send[lo:hi, :, at] = res.reshape(hi - lo, CAP, 256).astype(BF16)
            back = lax.dot_general(gate_grad[r0:r1, :], w[0], nt, preferred_element_type=F32)
            back = back + lax.dot_general(up_grad[r0:r1, :], w[1], nt, preferred_element_type=F32)
            back_send[lo:hi, :, at] = back.reshape(hi - lo, CAP, 256).astype(BF16)
            return 0

        lax.fori_loop(0, width // 256, outer, 0)
        for slot in range(max(lo, 1), hi):
            for a, (src, dst) in enumerate(((res_send, res_recv), (back_send, back_recv))):
                ret[a, slot] = send(
                    src.at[slot], dst.at[slot], ret_s.at[a, slot], ret_r.at[a, slot], peer(slot, -1)
                )
        if lo == 0:
            res_recv[0] = res_send[0]
            back_recv[0] = back_send[0]

    for lo, hi in CHUNKS:
        experts(lo, hi)

    def terms(i, _):
        at = pl.ds(pl.multiple_of(i * 256, 256), 256)
        for j, (left, right) in enumerate(((rows, gate_grad), (rows, up_grad), (grads, act))):
            got = lax.dot_general(left[:, at], right[...], tn, preferred_element_type=F32)
            term[pl.ds(2 * i, 2), j] = got.reshape(2, 128, hidden).astype(BF16)
        return 0

    lax.fori_loop(0, width // 256, terms, 0)

    rs = {}

    def reduce_send(half, index, at, which, axis, step):
        rs[half, index] = send(
            term.at[at, :, part(which, half), :], reduced.at[half, index],
            rs_s.at[half, index], rs_r.at[half, index], near(axis, step),
        )

    def add_into(half, at, which, indices):
        rows_at = part(which, half)
        for j in range(3):
            total = term[at, j, rows_at, :].astype(F32)
            for index in indices:
                total = total + reduced[half, index, j].astype(F32)
            term[at, j, rows_at, :] = total.astype(BF16)

    def ring(half, base, axis, at):
        def start():
            reduce_send(half, base + 0, at(2), "q", axis, 1)
            reduce_send(half, base + 1, at(2), "p", axis, -1)
            reduce_send(half, base + 2, at(1), "p", axis, 1)
            reduce_send(half, base + 3, at(-1), "q", axis, -1)

        def forward():
            rs[half, base + 0].wait_recv()
            add_into(half, at(1), "q", (base + 0,))
            reduce_send(half, base + 4, at(1), "q", axis, 1)
            rs[half, base + 1].wait_recv()
            add_into(half, at(-1), "p", (base + 1,))
            reduce_send(half, base + 5, at(-1), "p", axis, -1)

        def finish():
            for index in (2, 5):
                rs[half, base + index].wait_recv()
            add_into(half, at(0), "p", (base + 2, base + 5))
            for index in (3, 4):
                rs[half, base + index].wait_recv()
            add_into(half, at(0), "q", (base + 3, base + 4))

        return start, forward, finish

    first = {}
    ORDER = (2, 1, -1, 0)
    for k, i in enumerate(ORDER):
        for half in (0, 1):
            first[half, k] = ring(
                half, 6 * k, 1 if half == 0 else 0, functools.partial(block, half, i)
            )
    second = {
        half: ring(half, 24, 0 if half == 0 else 1, lambda j, half=half: block(half, j, 0))
        for half in (0, 1)
    }
    for stage in (0, 1):
        for k in range(4):
            for half in (0, 1):
                first[half, k][stage]()
    for k in range(4):
        for half in (0, 1):
            first[half, k][2]()
    for stage in (0, 1, 2):
        for half in (0, 1):
            second[half][stage]()
    weight_grad[...] = term[mine]

    for slot in range(1, SLOTS):
        for a in (0, 1):
            ret[a, slot].wait_recv()

    def combine(i, _):
        at = pl.ds(pl.multiple_of(i * 256, 256), 256)
        for table, source, to in ((weigh, res_recv, moe_out), (pick, back_recv, token_grad)):
            got = source[:, :, at].astype(F32).reshape(ROWS, 256).astype(BF16)
            to[:, at] = lax.dot_general(table[...], got, tn, preferred_element_type=F32).astype(BF16)
        return 0

    lax.fori_loop(0, width // 256, combine, 0)
    for copy in sent:
        copy.wait_send()


def on_device(tokens, expert_ids, gate_units, expert_weights, out_grad):
    count, width = tokens.shape
    _, part, kinds, hidden = expert_weights.shape
    blocks = width // part
    vmem = pl.BlockSpec(memory_space=pltpu.VMEM)
    slots = pltpu.VMEM((SLOTS, CAP, width), BF16)
    sem = pltpu.SemaphoreType.DMA
    moe_out, token_grad, weight_grad = pl.pallas_call(
        kernel,
        out_shape=(
            jax.ShapeDtypeStruct((count, width), BF16),
            jax.ShapeDtypeStruct((count, width), BF16),
            jax.ShapeDtypeStruct((kinds, part, hidden), BF16),
        ),
        in_specs=[vmem] * 5,
        out_specs=(vmem, vmem, vmem),
        scratch_shapes=[
            pltpu.VMEM((blocks, kinds, part, hidden), BF16),
            pltpu.VMEM((blocks, kinds, part, hidden), BF16),
            pltpu.VMEM((2, 30, kinds, part // 4, hidden), BF16),
            *([slots] * 8),
            *([pltpu.VMEM((ROWS, width), BF16)] * 2),
            *([pltpu.VMEM((ROWS, hidden), BF16)] * 3),
            *([pltpu.VMEM((ROWS, count), BF16)] * 2),
            sem((2, SLOTS)), sem((2, SLOTS)), sem((2, SLOTS)), sem((2, SLOTS)),
            sem((2, 20)), sem((2, 20)), sem((2, 30)), sem((2, 30)),
        ],
        compiler_params=pltpu.CompilerParams(
            collective_id=0, has_side_effects=True, vmem_limit_bytes=62 * 1024 * 1024
        ),
        name="experts",
    )(tokens, expert_ids, gate_units, jnp.transpose(expert_weights[0], (1, 0, 2)), out_grad)
    return moe_out, token_grad, jnp.transpose(weight_grad, (1, 0, 2))[None]


def solution(mesh):
    rows = P(("dp", "fsdp", "expert"), None)
    split = P("expert", ("dp", "fsdp"), None, None)
    return jax.shard_map(
        on_device,
        mesh=mesh,
        in_specs=(rows, rows, rows, split, rows),
        out_specs=(rows, rows, split),
        check_vma=False,
    )
```

time: 474 us -> 164 us (0.35)
  waiting for transfers between devices: 346 us -> 0 us
  Pallas kernels: 0 us -> 156 us
  matrix products: 37 us -> 0 us
  starting transfers between devices: 35.6 us -> 0 us
  other arithmetic: 18.8 us -> 0 us
  between operations: 14.2 us -> 0.66 us
  local copies, waits for them, and re-layouts: 18.5 us -> 6.94 us
    pallas_call x0 -> x1, Pallas kernels: none -> 156 us  [on_device(): pl.pallas_call(kernel, out_shape=(jax.ShapeDtypeStruct((count, width), BF...]
    all_to_all x5 -> x0, waiting for transfers between devices: 135 us -> none  [the longest x1 34.7 us: on_device(): lax.all_to_all(send_rows, 'expert', split_axis=0, concat_axis=0, tiled=True)]
    reduce_scatter x1 -> x0, waiting for transfers between devices: 112 us -> none  [on_device(): lax.psum_scatter(jnp.concatenate([input_term, down_term], axis=1).reshape...]
    all_gather x1 -> x0, waiting for transfers between devices: 99.4 us -> none  [on_device(): lax.all_gather(expert_weights, ('dp', 'fsdp'), axis=1, tiled=True)]
    dot_general x10 -> x0, matrix products: 37 us -> none  [the longest x1 6.93 us: on_device(): lax.dot_general(pair_grad, flat_weights[:, :2 * hidden_units], (((1,), (1...]
    all_to_all x5 -> x0, starting transfers between devices: 35.4 us -> none  [the longest x1 8.97 us: on_device(): lax.all_to_all(result.reshape(expert_count, CAP, model_width), 'expert',...]
    convert_element_type x3 -> x0, local copies, waits for them, and re-layouts: 13.5 us -> none  [the longest x1 12.7 us: on_device(): summed = lax.psum_scatter(jnp.concatenate([input_term, down_term], axis=1...]
    concatenate x1 -> x0, other arithmetic: 11.5 us -> none  [on_device(): jnp.concatenate([input_term, down_term], axis=1)]
  transfers between devices with their start and end apart: 7 -> 0, of which waited for: 7 -> 0; matrix products, arithmetic and copies ran while one was open for 7% -> 0% of each run, Pallas kernels for 0% -> 0%
where the time goes in v1:
time: 164 us
  Pallas kernels  156 us (95%)
  local copies, waits for them, and re-layouts  6.94 us (4%)
    pallas_call x1, Pallas kernels, on_device(): pl.pallas_call(kernel, out_shape=(jax.ShapeDtypeStruct((count, width), BF...  156 us
    unnamed x11, local copies, waits for them, and re-layouts  6.94 us

profile of v1, /device:TPU:33, one launch (start us, length us, event | category | flops | bytes accessed | tf_op | source)
XLA Modules:
  0.0 163.6 jit_solution(11078015977757629514)
XLA Ops:
  0.6 0.0 copy-start.2
  0.6 1.5 copy.8.ids
  2.1 0.0 copy-done.2
  2.1 0.8 copy.9.units
  2.9 156.0 %experts.1 = (bf16[256,2048]{1,0:T(8,128)(2,1)}, bf16[256,2048]{1,0:T(8,128)(2,1)}, bf16[3,128,768]{2,1,0:T(8,128)(2,1)}) custom-call(bf16[256,2048]{1,0:T(8,128)(2,1)} %tokens.1, s32[256,8]{1,0:T(8,128)} %copy.8.ids, s32[256,8]{1,0:T(8,128)} %copy.9.units, bf16[3,128,768]{2,1,0:T(8,128)(2,1)} %bitcast.7, bf16[256,2048]{1,0:T(8,128)(2,1)} %out_grad.1), custom_call_target="tpu_custom_call" | custom-call | tf_op jit(solution)/shard_map/experts/pallas_call | solution.py:344
  158.9 0.0 copy-start
  158.9 2.4 %copy.13 = bf16[256,2048]{1,0:T(8,128)(2,1)} copy(bf16[256,2048]{1,0:T(8,128)(2,1)} %get-tuple-element.12) | data formatting | bytes 2097152
  161.3 0.0 copy-done
  161.3 0.0 copy-start.1
  161.3 1.0 copy.14
  162.3 0.5 copy-done.1
  162.8 0.8 copy.15
Async XLA Ops:
  0.6 1.5 copy-start.2
  158.9 2.4 %copy-start = (bf16[256,2048]{1,0:T(8,128)(2,1)S(1)}, bf16[256,2048]{1,0:T(8,128)(2,1)}, u32[]{:S(2)}) copy-start(bf16[256,2048]{1,0:T(8,128)(2,1)} %get-tuple-element.13) | copy-start | bytes 3145732
  161.3 1.4 copy-start.1

commit v2 on v1

--- a/solution.py
+++ b/solution.py
@@ -16,7 +16,7 @@
 
 OFFSETS = [(dz, dc) for dz in (0, 1, 7, 2, 6, 3, 5, 4) for dc in (0, 1)]
 CHUNKS = ((0, 10), (10, 14), (14, 16))
-PIECES = ((0, 6), (6, 10), (10, 14), (14, 16))
+PIECES = ((2, 6), (6, 10), (10, 14), (14, 16), (0, 2))
 
 
 def place():
@@ -29,16 +29,17 @@
 
 
 def kernel(
-    tokens, ids, units, weights, out_grad,
+    tokens_in, ids, units, weights, out_grad_in,
     moe_out, token_grad, weight_grad,
     full, term, reduced, row_send, grad_send, row_recv, grad_recv,
     res_send, back_send, res_recv, back_recv, rows, grads, act, gate_grad, up_grad,
-    pick, weigh,
-    out_s, out_r, ret_s, ret_r, ag_s, ag_r, rs_s, rs_r,
+    pick, weigh, tokens, out_grad, moe_sum, grad_sum,
+    out_s, out_r, ret_s, ret_r, ag_s, ag_r, rs_s, rs_r, in_s, done_s,
 ):
     x, y, z, core = place()
     width = tokens.shape[1]
     hidden = weights.shape[2]
+    token_count = tokens.shape[0]
 
     def peer(slot, sign):
         dz, dc = OFFSETS[slot]
@@ -62,7 +63,38 @@
             pl.semaphore_signal(barrier, inc=1, device_id=near(axis, step), device_id_type=MESH)
 
     mine = block(0, 0, 0)
-    full[mine] = weights[...]
+    loads = [
+        pltpu.make_async_copy(src, dst, in_s.at[i])
+        for i, (src, dst) in enumerate(
+            ((tokens_in, tokens), (weights, full.at[mine]), (out_grad_in, out_grad))
+        )
+    ]
+    for load in loads:
+        load.start()
+
+    shape = (ROWS, token_count)
+    row = lax.broadcasted_iota(jnp.int32, shape, 0)
+    slot_of = (row * 2731) >> 16
+    rank_of = (row - slot_of * CAP).astype(F32)
+    pair = slot_of >> 1
+    dz = jnp.where((pair & 1) == 1, (pair + 1) >> 1, (8 - (pair >> 1)) & 7)
+    named = ((z + dz) & 7) * 2 + ((core + slot_of) & 1)
+    chosen = jnp.zeros(shape, F32)
+    for k in range(ids.shape[0]):
+        chosen = chosen + jnp.where(
+            ids[k : k + 1, :] == named, units[k : k + 1, :].astype(F32), 0.0
+        )
+    earlier = (
+        lax.broadcasted_iota(jnp.int32, (token_count, token_count), 0)
+        < lax.broadcasted_iota(jnp.int32, (token_count, token_count), 1)
+    ).astype(F32).astype(BF16)
+    ranking = jnp.dot(
+        (chosen > 0.0).astype(F32).astype(BF16), earlier, preferred_element_type=F32
+    )
+    gate = jnp.where(ranking == rank_of, chosen, 0.0)
+    weigh[...] = (gate * (1.0 / 256.0)).astype(BF16)
+    pick[...] = (gate > 0.0).astype(F32).astype(BF16)
+
     pl.semaphore_wait(barrier, SLOTS - 1 + 4)
 
     sent = []
@@ -113,68 +145,45 @@
         ag[half, 5 + 4 * k].wait_recv()
         gather_send(half, 7 + 4 * k, block(half, ITEMS[k], 1), "q", a2, -1)
 
+    loads[1].wait()
     for half in (0, 1):
         gather_own(half)
     for half in (0, 1):
         gather_item(half, 0)
-
-    lane = lax.broadcasted_iota(jnp.int32, (1, ROWS), 1)
-    slot_of = jnp.zeros((1, ROWS), jnp.int32)
-    for j in range(1, SLOTS):
-        slot_of = slot_of + (lane >= CAP * j).astype(jnp.int32)
-    rank_of = (lane - slot_of * CAP).astype(F32)
-    pair = slot_of >> 1
-    dz = jnp.where((pair & 1) == 1, (pair + 1) >> 1, (8 - (pair >> 1)) & 7)
-    named = ((z + dz) & 7) * 2 + ((core + (slot_of & 1)) & 1)
-    token_count = tokens.shape[0]
-    chosen = jnp.zeros((token_count, ROWS), F32)
-    id_table = ids[...]
-    unit_table = units[...].astype(F32)
-    for k in range(ids.shape[1]):
-        chosen = chosen + jnp.where(id_table[:, k : k + 1] == named, unit_table[:, k : k + 1], 0.0)
-    earlier = (
-        lax.broadcasted_iota(jnp.int32, (token_count, token_count), 1)
-        < lax.broadcasted_iota(jnp.int32, (token_count, token_count), 0)
-    ).astype(F32).astype(BF16)
-    ranking = jnp.dot(
-        earlier, (chosen > 0.0).astype(F32).astype(BF16), preferred_element_type=F32
-    )
-    gate = jnp.where(ranking == rank_of, chosen, 0.0)
-    weigh[...] = (jnp.transpose(gate) * (1.0 / 256.0)).astype(BF16)
-    pick[...] = jnp.transpose((gate > 0.0).astype(F32)).astype(BF16)
 
     out = {}
 
     def dispatch(lo, hi):
         cols = 512
-
-        def tile(i, _):
-            at = pl.ds(pl.multiple_of(i * cols, cols), cols)
-            for table, source, to in ((pick, tokens, row_send), (weigh, out_grad, grad_send)):
+        for a, (table, source, src, dst) in enumerate(
+            ((pick, tokens, row_send, row_recv), (weigh, out_grad, grad_send, grad_recv))
+        ):
+            if (lo, hi) == PIECES[0]:
+                loads[2 * a].wait()
+
+            def tile(i, _, table=table, source=source, src=src):
+                at = pl.ds(pl.multiple_of(i * cols, cols), cols)
                 got = jnp.dot(
                     table[CAP * lo : CAP * hi, :], source[:, at], preferred_element_type=F32
                 )
-                to[lo:hi, :, at] = got.reshape(hi - lo, CAP, cols).astype(BF16)
-            return 0
-
-        lax.fori_loop(0, width // cols, tile, 0)
-        for slot in range(max(lo, 1), hi):
-            for a, (src, dst) in enumerate(((row_send, row_recv), (grad_send, grad_recv))):
+                src[lo:hi, :, at] = got.reshape(hi - lo, CAP, cols).astype(BF16)
+                return 0
+
+            lax.fori_loop(0, width // cols, tile, 0)
+            for slot in range(max(lo, 1), hi):
                 out[a, slot] = send(
                     src.at[slot], dst.at[slot], out_s.at[a, slot], out_r.at[a, slot], peer(slot, 1)
                 )
-
-    dispatch(*PIECES[0])
-    row_recv[0] = row_send[0]
-    grad_recv[0] = grad_send[0]
-    dispatch(*PIECES[1])
+            if lo == 0:
+                dst[0] = src[0]
+
+    for piece in PIECES:
+        dispatch(*piece)
     for half in (0, 1):
         gather_forward_first(half)
     for half in (0, 1):
         gather_item(half, 1)
         gather_item(half, 2)
-    dispatch(*PIECES[2])
-    dispatch(*PIECES[3])
     for half in (0, 1):
         gather_forward_item(half, 0)
     for half in (0, 1):
@@ -306,32 +315,84 @@
         half: ring(half, 24, 0 if half == 0 else 1, lambda j, half=half: block(half, j, 0))
         for half in (0, 1)
     }
+    tables = ((weigh, res_recv, moe_sum, tokens, moe_out), (pick, back_recv, grad_sum, out_grad, token_grad))
+
+    def combine(n):
+        lo, hi = CHUNKS[n]
+        r0, r1 = CAP * lo, CAP * hi
+        for slot in range(max(lo, 1), hi):
+            for a in (0, 1):
+                ret[a, slot].wait_recv()
+
+        def tile(i, _):
+            at = pl.ds(pl.multiple_of(i * 256, 256), 256)
+            for table, source, total, result, _ in tables:
+                got = source[lo:hi, :, at].astype(F32).reshape(r1 - r0, 256).astype(BF16)
+                value = lax.dot_general(table[r0:r1, :], got, tn, preferred_element_type=F32)
+                if n > 0:
+                    value = total[:, at] + value
+                if hi < SLOTS:
+                    total[:, at] = value
+                else:
+                    result[:, at] = value.astype(BF16)
+            return 0
+
+        if hi < SLOTS:
+            lax.fori_loop(0, width // 256, tile, 0)
+            return
+        per = width // 256 // 4
+        for part in range(4):
+            lax.fori_loop(part * per, (part + 1) * per, tile, 0)
+            at = pl.ds(part * per * 256, per * 256)
+            for a, (_, _, _, result, to) in enumerate(tables):
+                copy = pltpu.make_async_copy(result.at[:, at], to.at[:, at], done_s.at[a, part])
+                copy.start()
+                finals.append(copy)
+
+    finals = []
     for stage in (0, 1):
         for k in range(4):
             for half in (0, 1):
                 first[half, k][stage]()
+    combine(0)
     for k in range(4):
         for half in (0, 1):
             first[half, k][2]()
     for stage in (0, 1, 2):
         for half in (0, 1):
             second[half][stage]()
-    weight_grad[...] = term[mine]
-
-    for slot in range(1, SLOTS):
-        for a in (0, 1):
-            ret[a, slot].wait_recv()
-
-    def combine(i, _):
-        at = pl.ds(pl.multiple_of(i * 256, 256), 256)
-        for table, source, to in ((weigh, res_recv, moe_out), (pick, back_recv, token_grad)):
-            got = source[:, :, at].astype(F32).reshape(ROWS, 256).astype(BF16)
-            to[:, at] = lax.dot_general(table[...], got, tn, preferred_element_type=F32).astype(BF16)
-        return 0
-
-    lax.fori_loop(0, width // 256, combine, 0)
+    copy = pltpu.make_async_copy(term.at[mine], weight_grad, done_s.at[2, 0])
+    copy.start()
+    finals.append(copy)
+    combine(1)
+    combine(2)
+    for copy in finals:
+        copy.wait()
     for copy in sent:
         copy.wait_send()
+
+
+def hand_out(*refs):
+    sources, targets, (held_a, held_b, held_c, sems) = refs[:3], refs[3:6], refs[6:]
+    steps = []
+    for i, (src, held, dst) in enumerate(zip(sources, (held_a, held_b, held_c), targets)):
+        parts = 4 if src.shape[0] % 4 == 0 else 3
+        size = src.shape[0] // parts
+        for k in range(parts):
+            at = pl.ds(k * size, size)
+            steps.append(
+                (
+                    pltpu.make_async_copy(src.at[at], held.at[at], sems.at[0, i, k]),
+                    pltpu.make_async_copy(held.at[at], dst.at[at], sems.at[1, i, k]),
+                )
+            )
+    for load, _ in steps:
+        load.start()
+    for load, store in steps:
+        load.wait()
+        store.start()
+    for _, store in steps:
+        store.wait()
 
 
 def on_device(tokens, expert_ids, gate_units, expert_weights, out_grad):
@@ -339,17 +400,19 @@
     _, part, kinds, hidden = expert_weights.shape
     blocks = width // part
     vmem = pl.BlockSpec(memory_space=pltpu.VMEM)
+    anywhere = pl.BlockSpec(memory_space=pl.ANY)
     slots = pltpu.VMEM((SLOTS, CAP, width), BF16)
     sem = pltpu.SemaphoreType.DMA
-    moe_out, token_grad, weight_grad = pl.pallas_call(
+    shapes = (
+        jax.ShapeDtypeStruct((count, width), BF16),
+        jax.ShapeDtypeStruct((count, width), BF16),
+        jax.ShapeDtypeStruct((kinds, part, hidden), BF16),
+    )
+    results = pl.pallas_call(
         kernel,
-        out_shape=(
-            jax.ShapeDtypeStruct((count, width), BF16),
-            jax.ShapeDtypeStruct((count, width), BF16),
-            jax.ShapeDtypeStruct((kinds, part, hidden), BF16),
-        ),
-        in_specs=[vmem] * 5,
-        out_specs=(vmem, vmem, vmem),
+        out_shape=shapes,
+        in_specs=[anywhere, vmem, vmem, anywhere, anywhere],
+        out_specs=(anywhere,) * 3,
         scratch_shapes=[
             pltpu.VMEM((blocks, kinds, part, hidden), BF16),
             pltpu.VMEM((blocks, kinds, part, hidden), BF16),
@@ -358,14 +421,24 @@
             *([pltpu.VMEM((ROWS, width), BF16)] * 2),
             *([pltpu.VMEM((ROWS, hidden), BF16)] * 3),
             *([pltpu.VMEM((ROWS, count), BF16)] * 2),
+            *([pltpu.VMEM((count, width), BF16)] * 2),
+            *([pltpu.VMEM((count, width), F32)] * 2),
             sem((2, SLOTS)), sem((2, SLOTS)), sem((2, SLOTS)), sem((2, SLOTS)),
-            sem((2, 20)), sem((2, 20)), sem((2, 30)), sem((2, 30)),
+            sem((2, 20)), sem((2, 20)), sem((2, 30)), sem((2, 30)), sem((3,)), sem((3, 4)),
         ],
         compiler_params=pltpu.CompilerParams(
             collective_id=0, has_side_effects=True, vmem_limit_bytes=62 * 1024 * 1024
         ),
         name="experts",
-    )(tokens, expert_ids, gate_units, jnp.transpose(expert_weights[0], (1, 0, 2)), out_grad)
+    )(tokens, expert_ids.T, gate_units.T, jnp.transpose(expert_weights[0], (1, 0, 2)), out_grad)
+    moe_out, token_grad, weight_grad = pl.pallas_call(
+        hand_out,
+        out_shape=shapes,
+        in_specs=[anywhere] * 3,
+        out_specs=(anywhere,) * 3,
+        scratch_shapes=[*(pltpu.VMEM(a.shape, a.dtype) for a in shapes), sem((2, 3, 4))],
+        name="hand_out",
+    )(*results)
     return moe_out, token_grad, jnp.transpose(weight_grad, (1, 0, 2))[None]
 
 

time: 164 us -> 157 us (0.957)
  local copies, waits for them, and re-layouts: 6.94 us -> 0 us
    unnamed x11 -> x0, local copies, waits for them, and re-layouts: 6.94 us -> none
    pallas_call x1 -> x2, Pallas kernels: 156 us -> 156 us  [the longest x1 153 us: on_device(): pl.pallas_call(kernel, out_shape=shapes, in_specs=[anywhere, vmem, vmem,...]
where the time goes in v2:
time: 157 us
  Pallas kernels  156 us (99%)
    pallas_call x1, Pallas kernels, on_device(): pl.pallas_call(kernel, out_shape=shapes, in_specs=[anywhere, vmem, vmem,...  153 us

profile of v2, /device:TPU:33, one launch (start us, length us, event | category | flops | bytes accessed | tf_op | source)
XLA Modules:
  0.0 156.7 jit_solution(9200400029598224782)
XLA Ops:
  0.6 153.4 %experts.1 = (bf16[256,2048]{1,0:T(8,128)(2,1)}, bf16[256,2048]{1,0:T(8,128)(2,1)}, bf16[3,128,768]{2,1,0:T(8,128)(2,1)}) custom-call(bf16[256,2048]{1,0:T(8,128)(2,1)} %tokens_in.1, s32[8,256]{1,0:T(8,128)} %bitcast.9, s32[8,256]{1,0:T(8,128)} %bitcast.10, bf16[3,128,768]{2,1,0:T(8,128)(2,1)} %bitcast.8, bf16[256,2048]{1,0:T(8,128)(2,1)} %out_grad_in.1), custom_call_target="tpu_custom_call" | custom-call | tf_op jit(solution)/shard_map/experts/pallas_call | solution.py:411
  154.0 2.7 %hand_out.1 = (bf16[256,2048]{1,0:T(8,128)(2,1)}, bf16[256,2048]{1,0:T(8,128)(2,1)}, bf16[3,128,768]{2,1,0:T(8,128)(2,1)}) custom-call(bf16[256,2048]{1,0:T(8,128)(2,1)} %get-tuple-element.9.refs_0_, bf16[256,2048]{1,0:T(8,128)(2,1)} %get-tuple-element.10.refs_1_, bf16[3,128,768]{2,1,0:T(8,128)(2,1)} %get-tuple-element.11.refs_2_), custom_call_target="tpu_custom_call" | custom-call | tf_op jit(solution)/shard_map/hand_out/pallas_call | solution.py:434

commit v3 on v2

--- a/solution.py
+++ b/solution.py
@@ -33,8 +33,8 @@
     moe_out, token_grad, weight_grad,
     full, term, reduced, row_send, grad_send, row_recv, grad_recv,
     res_send, back_send, res_recv, back_recv, rows, grads, act, gate_grad, up_grad,
-    pick, weigh, tokens, out_grad, moe_sum, grad_sum,
-    out_s, out_r, ret_s, ret_r, ag_s, ag_r, rs_s, rs_r, in_s, done_s,
+    pick, weigh, tokens, out_grad, moe_sum, grad_sum, spread_a, spread_b, spread_c,
+    out_s, out_r, ret_s, ret_r, ag_s, ag_r, rs_s, rs_r, in_s,
 ):
     x, y, z, core = place()
     width = tokens.shape[1]
@@ -169,7 +169,7 @@
                 src[lo:hi, :, at] = got.reshape(hi - lo, CAP, cols).astype(BF16)
                 return 0
 
-            lax.fori_loop(0, width // cols, tile, 0)
+            lax.fori_loop(0, width // cols, tile, 0, unroll=(lo, hi) == PIECES[0])
             for slot in range(max(lo, 1), hi):
                 out[a, slot] = send(
                     src.at[slot], dst.at[slot], out_s.at[a, slot], out_r.at[a, slot], peer(slot, 1)
@@ -179,6 +179,10 @@
 
     for piece in PIECES:
         dispatch(*piece)
+    spread = (spread_a, spread_b, spread_c)
+    for (lo, hi), to in zip(CHUNKS, spread):
+        for a, table in enumerate((weigh, pick)):
+            to[a] = jnp.transpose(table[CAP * lo : CAP * hi, :].astype(F32)).astype(BF16)
     for half in (0, 1):
         gather_forward_first(half)
     for half in (0, 1):
@@ -315,20 +319,19 @@
         half: ring(half, 24, 0 if half == 0 else 1, lambda j, half=half: block(half, j, 0))
         for half in (0, 1)
     }
-    tables = ((weigh, res_recv, moe_sum, tokens, moe_out), (pick, back_recv, grad_sum, out_grad, token_grad))
+    tables = ((res_recv, moe_sum, moe_out), (back_recv, grad_sum, token_grad))
 
     def combine(n):
         lo, hi = CHUNKS[n]
-        r0, r1 = CAP * lo, CAP * hi
         for slot in range(max(lo, 1), hi):
             for a in (0, 1):
                 ret[a, slot].wait_recv()
 
         def tile(i, _):
-            at = pl.ds(pl.multiple_of(i * 256, 256), 256)
-            for table, source, total, result, _ in tables:
-                got = source[lo:hi, :, at].astype(F32).reshape(r1 - r0, 256).astype(BF16)
-                value = lax.dot_general(table[r0:r1, :], got, tn, preferred_element_type=F32)
+            at = pl.ds(pl.multiple_of(i * 512, 512), 512)
+            for a, (source, total, result) in enumerate(tables):
+                got = source[lo:hi, :, at].astype(F32).reshape(CAP * (hi - lo), 512).astype(BF16)
+                value = jnp.dot(spread[n][a], got, preferred_element_type=F32)
                 if n > 0:
                     value = total[:, at] + value
                 if hi < SLOTS:
@@ -337,19 +340,8 @@
                     result[:, at] = value.astype(BF16)
             return 0
 
-        if hi < SLOTS:
-            lax.fori_loop(0, width // 256, tile, 0)
-            return
-        per = width // 256 // 4
-        for part in range(4):
-            lax.fori_loop(part * per, (part + 1) * per, tile, 0)
-            at = pl.ds(part * per * 256, per * 256)
-            for a, (_, _, _, result, to) in enumerate(tables):
-                copy = pltpu.make_async_copy(result.at[:, at], to.at[:, at], done_s.at[a, part])
-                copy.start()
-                finals.append(copy)
-
-    finals = []
+        lax.fori_loop(0, width // 512, tile, 0, unroll=hi == SLOTS)
+
     for stage in (0, 1):
         for k in range(4):
             for half in (0, 1):
@@ -361,38 +353,26 @@
     for stage in (0, 1, 2):
         for half in (0, 1):
             second[half][stage]()
-    copy = pltpu.make_async_copy(term.at[mine], weight_grad, done_s.at[2, 0])
-    copy.start()
-    finals.append(copy)
+    weight_grad[...] = term[mine]
     combine(1)
     combine(2)
-    for copy in finals:
-        copy.wait()
     for copy in sent:
         copy.wait_send()
 
 
 def hand_out(*refs):
-    sources, targets, (held_a, held_b, held_c, sems) = refs[:3], refs[3:6], refs[6:]
-    steps = []
-    for i, (src, held, dst) in enumerate(zip(sources, (held_a, held_b, held_c), targets)):
+    sources, targets, sems = refs[:3], refs[3:6], refs[6]
+    copies = []
+    for i, (src, dst) in enumerate(zip(sources, targets)):
         parts = 4 if src.shape[0] % 4 == 0 else 3
         size = src.shape[0] // parts
         for k in range(parts):
             at = pl.ds(k * size, size)
-            steps.append(
-                (
-                    pltpu.make_async_copy(src.at[at], held.at[at], sems.at[0, i, k]),
-                    pltpu.make_async_copy(held.at[at], dst.at[at], sems.at[1, i, k]),
-                )
-            )
-    for load, _ in steps:
-        load.start()
-    for load, store in steps:
-        load.wait()
-        store.start()
-    for _, store in steps:
-        store.wait()
+            copies.append(pltpu.make_async_copy(src.at[at], dst.at[at], sems.at[i, k]))
+    for copy in copies:
+        copy.start()
+    for copy in copies:
+        copy.wait()
 
 
 def on_device(tokens, expert_ids, gate_units, expert_weights, out_grad):
@@ -410,9 +390,9 @@
     )
     results = pl.pallas_call(
         kernel,
-        out_shape=shapes,
+        out_shape=tuple(pltpu.VMEM(a.shape, a.dtype) for a in shapes),
         in_specs=[anywhere, vmem, vmem, anywhere, anywhere],
-        out_specs=(anywhere,) * 3,
+        out_specs=(vmem,) * 3,
         scratch_shapes=[
             pltpu.VMEM((blocks, kinds, part, hidden), BF16),
             pltpu.VMEM((blocks, kinds, part, hidden), BF16),
@@ -423,11 +403,12 @@
             *([pltpu.VMEM((ROWS, count), BF16)] * 2),
             *([pltpu.VMEM((count, width), BF16)] * 2),
             *([pltpu.VMEM((count, width), F32)] * 2),
+            *(pltpu.VMEM((2, count, CAP * (hi - lo)), BF16) for lo, hi in CHUNKS),
             sem((2, SLOTS)), sem((2, SLOTS)), sem((2, SLOTS)), sem((2, SLOTS)),
-            sem((2, 20)), sem((2, 20)), sem((2, 30)), sem((2, 30)), sem((3,)), sem((3, 4)),
+            sem((2, 20)), sem((2, 20)), sem((2, 30)), sem((2, 30)), sem((3,)),
         ],
         compiler_params=pltpu.CompilerParams(
-            collective_id=0, has_side_effects=True, vmem_limit_bytes=62 * 1024 * 1024
+            collective_id=0, has_side_effects=True, vmem_limit_bytes=57 * 1024 * 1024
         ),
         name="experts",
     )(tokens, expert_ids.T, gate_units.T, jnp.transpose(expert_weights[0], (1, 0, 2)), out_grad)
@@ -436,9 +417,9 @@
         out_shape=shapes,
         in_specs=[anywhere] * 3,
         out_specs=(anywhere,) * 3,
-        scratch_shapes=[*(pltpu.VMEM(a.shape, a.dtype) for a in shapes), sem((2, 3, 4))],
+        scratch_shapes=[sem((3, 4))],
         name="hand_out",
-    )(*results)
+    )(*(pltpu.with_memory_space_constraint(a, pltpu.VMEM) for a in results))
     return moe_out, token_grad, jnp.transpose(weight_grad, (1, 0, 2))[None]
 
 

time: 157 us -> 153 us (0.975)
  Pallas kernels: 156 us -> 151 us
    pallas_call x1, Pallas kernels: 153 us -> 150 us  [on_device(): pl.pallas_call(kernel, out_shape=tuple((pltpu.VMEM(a.shape, a.dtype) for...]
where the time goes in v3:
time: 153 us; the launch traced here: 152 us
  Pallas kernels  151 us (99%)
    pallas_call x1, Pallas kernels, on_device(): pl.pallas_call(kernel, out_shape=tuple((pltpu.VMEM(a.shape, a.dtype) for...  150 us

profile of v3, /device:TPU:33, one launch (start us, length us, event | category | flops | bytes accessed | tf_op | source)
XLA Modules:
  0.0 152.1 jit_solution(5730590222424255169)
XLA Ops:
  0.6 149.8 %experts.1 = (bf16[256,2048]{1,0:T(8,128)(2,1)S(1)}, bf16[256,2048]{1,0:T(8,128)(2,1)S(1)}, bf16[3,128,768]{2,1,0:T(8,128)(2,1)S(1)}) custom-call(bf16[256,2048]{1,0:T(8,128)(2,1)} %tokens_in.1, s32[8,256]{1,0:T(8,128)} %bitcast.9, s32[8,256]{1,0:T(8,128)} %bitcast.10, bf16[3,128,768]{2,1,0:T(8,128)(2,1)} %bitcast.8, bf16[256,2048]{1,0:T(8,128)(2,1)} %out_grad_in.1), custom_call_target="tpu_custom_call" | custom-call | tf_op jit(solution)/shard_map/experts/pallas_call | solution.py:391
  150.5 1.6 %hand_out.1 = (bf16[256,2048]{1,0:T(8,128)(2,1)}, bf16[256,2048]{1,0:T(8,128)(2,1)}, bf16[3,128,768]{2,1,0:T(8,128)(2,1)}) custom-call(bf16[256,2048]{1,0:T(8,128)(2,1)S(1)} %get-tuple-element.9.refs_0_, bf16[256,2048]{1,0:T(8,128)(2,1)S(1)} %get-tuple-element.10.refs_1_, bf16[3,128,768]{2,1,0:T(8,128)(2,1)S(1)} %get-tuple-element.11.refs_2_), custom_call_target="tpu_custom_call" | custom-call | tf_op jit(solution)/shard_map/hand_out/pallas_call | solution.py:415

commit v4 on v3

--- a/solution.py
+++ b/solution.py
@@ -14,9 +14,11 @@
 BF16 = jnp.bfloat16
 F32 = jnp.float32
 
-OFFSETS = [(dz, dc) for dz in (0, 1, 7, 2, 6, 3, 5, 4) for dc in (0, 1)]
+STEPS = (0, 1, 7, 2, 6, 3, 5, 4)
+OFFSETS = [(dz, dc) for dz in STEPS for dc in (0, 1)]
+OWN = OFFSETS.index((0, 0))
 CHUNKS = ((0, 10), (10, 14), (14, 16))
-PIECES = ((2, 6), (6, 10), (10, 14), (14, 16), (0, 2))
+PIECES = ((2, 4), (4, 6), (6, 10), (10, 14), (14, 16), (0, 2))
 
 
 def place():
@@ -28,15 +30,21 @@
     return (lax.div(y, 2), x * 2 + lax.rem(y, 2), z * 2 + core)
 
 
+def others(lo, hi):
+    return [slot for slot in range(lo, hi) if slot != OWN]
+
+
 def kernel(
     tokens_in, ids, units, weights, out_grad_in,
     moe_out, token_grad, weight_grad,
-    full, term, reduced, row_send, grad_send, row_recv, grad_recv,
-    res_send, back_send, res_recv, back_recv, rows, grads, act, gate_grad, up_grad,
+    full, term, reduced, pair_send, pair_recv, ret_send, ret_recv, rows, grads, act, gate_grad, up_grad,
     pick, weigh, tokens, out_grad, moe_sum, grad_sum, spread_a, spread_b, spread_c,
     out_s, out_r, ret_s, ret_r, ag_s, ag_r, rs_s, rs_r, in_s,
 ):
     x, y, z, core = place()
+    (row_send, grad_send), (row_recv, grad_recv), (res_send, back_send), (res_recv, back_recv) = (
+        (ref.at[:, 0], ref.at[:, 1]) for ref in (pair_send, pair_recv, ret_send, ret_recv)
+    )
     width = tokens.shape[1]
     hidden = weights.shape[2]
     token_count = tokens.shape[0]
@@ -56,7 +64,7 @@
         return lax.div(by, 2) * 8 + bx * 2 + lax.rem(by, 2)
 
     barrier = pltpu.get_barrier_semaphore()
-    for slot in range(1, SLOTS):
+    for slot in others(0, SLOTS):
         pl.semaphore_signal(barrier, inc=1, device_id=peer(slot, 1), device_id_type=MESH)
     for axis in (0, 1):
         for step in (1, -1):
@@ -77,7 +85,9 @@
     slot_of = (row * 2731) >> 16
     rank_of = (row - slot_of * CAP).astype(F32)
     pair = slot_of >> 1
-    dz = jnp.where((pair & 1) == 1, (pair + 1) >> 1, (8 - (pair >> 1)) & 7)
+    dz = jnp.zeros(shape, jnp.int32)
+    for k, step in enumerate(STEPS):
+        dz = jnp.where(pair == k, step, dz)
     named = ((z + dz) & 7) * 2 + ((core + slot_of) & 1)
     chosen = jnp.zeros(shape, F32)
     for k in range(ids.shape[0]):
@@ -95,8 +105,6 @@
     weigh[...] = (gate * (1.0 / 256.0)).astype(BF16)
     pick[...] = (gate > 0.0).astype(F32).astype(BF16)
 
-    pl.semaphore_wait(barrier, SLOTS - 1 + 4)
-
     sent = []
 
     def send(src, dst, send_sem, recv_sem, to):
@@ -145,40 +153,48 @@
         ag[half, 5 + 4 * k].wait_recv()
         gather_send(half, 7 + 4 * k, block(half, ITEMS[k], 1), "q", a2, -1)
 
+    out = {}
+    routes = ((pick, tokens, row_send, row_recv), (weigh, out_grad, grad_send, grad_recv))
+
+    def choose(piece, a):
+        lo, hi = piece
+        cols = 512
+        table, source, src, _ = routes[a]
+        if piece == PIECES[0]:
+            loads[2 * a].wait()
+
+        def tile(i, _):
+            at = pl.ds(pl.multiple_of(i * cols, cols), cols)
+            got = jnp.dot(
+                table[CAP * lo : CAP * hi, :], source[:, at], preferred_element_type=F32
+            )
+            src[lo:hi, :, at] = got.reshape(hi - lo, CAP, cols).astype(BF16)
+            return 0
+
+        lax.fori_loop(0, width // cols, tile, 0, unroll=piece == PIECES[0])
+
+    def post(piece):
+        lo, hi = piece
+        for slot in others(lo, hi):
+            out[slot] = send(
+                pair_send.at[slot], pair_recv.at[slot], out_s.at[slot], out_r.at[slot], peer(slot, 1)
+            )
+        if lo <= OWN < hi:
+            pair_recv[OWN] = pair_send[OWN]
+
+    choose(PIECES[0], 0)
+    choose(PIECES[0], 1)
+    pl.semaphore_wait(barrier, SLOTS - 1 + 4)
+    post(PIECES[0])
     loads[1].wait()
     for half in (0, 1):
         gather_own(half)
     for half in (0, 1):
         gather_item(half, 0)
-
-    out = {}
-
-    def dispatch(lo, hi):
-        cols = 512
-        for a, (table, source, src, dst) in enumerate(
-            ((pick, tokens, row_send, row_recv), (weigh, out_grad, grad_send, grad_recv))
-        ):
-            if (lo, hi) == PIECES[0]:
-                loads[2 * a].wait()
-
-            def tile(i, _, table=table, source=source, src=src):
-                at = pl.ds(pl.multiple_of(i * cols, cols), cols)
-                got = jnp.dot(
-                    table[CAP * lo : CAP * hi, :], source[:, at], preferred_element_type=F32
-                )
-                src[lo:hi, :, at] = got.reshape(hi - lo, CAP, cols).astype(BF16)
-                return 0
-
-            lax.fori_loop(0, width // cols, tile, 0, unroll=(lo, hi) == PIECES[0])
-            for slot in range(max(lo, 1), hi):
-                out[a, slot] = send(
-                    src.at[slot], dst.at[slot], out_s.at[a, slot], out_r.at[a, slot], peer(slot, 1)
-                )
-            if lo == 0:
-                dst[0] = src[0]
-
-    for piece in PIECES:
-        dispatch(*piece)
+    for piece in PIECES[1:]:
+        choose(piece, 0)
+        choose(piece, 1)
+        post(piece)
     spread = (spread_a, spread_b, spread_c)
     for (lo, hi), to in zip(CHUNKS, spread):
         for a, table in enumerate((weigh, pick)):
@@ -208,9 +224,8 @@
 
     def experts(lo, hi):
         r0, r1 = CAP * lo, CAP * hi
-        for slot in range(max(lo, 1), hi):
-            for a in (0, 1):
-                out[a, slot].wait_recv()
+        for slot in others(lo, hi):
+            out[slot].wait_recv()
 
         def pack(i, _):
             at = pl.ds(pl.multiple_of(i * 512, 512), 512)
@@ -246,14 +261,12 @@
             return 0
 
         lax.fori_loop(0, width // 256, outer, 0)
-        for slot in range(max(lo, 1), hi):
-            for a, (src, dst) in enumerate(((res_send, res_recv), (back_send, back_recv))):
-                ret[a, slot] = send(
-                    src.at[slot], dst.at[slot], ret_s.at[a, slot], ret_r.at[a, slot], peer(slot, -1)
-                )
-        if lo == 0:
-            res_recv[0] = res_send[0]
-            back_recv[0] = back_send[0]
+        for slot in others(lo, hi):
+            ret[slot] = send(
+                ret_send.at[slot], ret_recv.at[slot], ret_s.at[slot], ret_r.at[slot], peer(slot, -1)
+            )
+        if lo <= OWN < hi:
+            ret_recv[OWN] = ret_send[OWN]
 
     for lo, hi in CHUNKS:
         experts(lo, hi)
@@ -321,23 +334,23 @@
     }
     tables = ((res_recv, moe_sum, moe_out), (back_recv, grad_sum, token_grad))
 
-    def combine(n):
+    def combine(n, a):
         lo, hi = CHUNKS[n]
-        for slot in range(max(lo, 1), hi):
-            for a in (0, 1):
-                ret[a, slot].wait_recv()
+        source, total, result = tables[a]
+        if a == 0:
+            for slot in others(lo, hi):
+                ret[slot].wait_recv()
 
         def tile(i, _):
             at = pl.ds(pl.multiple_of(i * 512, 512), 512)
-            for a, (source, total, result) in enumerate(tables):
-                got = source[lo:hi, :, at].astype(F32).reshape(CAP * (hi - lo), 512).astype(BF16)
-                value = jnp.dot(spread[n][a], got, preferred_element_type=F32)
-                if n > 0:
-                    value = total[:, at] + value
-                if hi < SLOTS:
-                    total[:, at] = value
-                else:
-                    result[:, at] = value.astype(BF16)
+            got = source[lo:hi, :, at].astype(F32).reshape(CAP * (hi - lo), 512).astype(BF16)
+            value = jnp.dot(spread[n][a], got, preferred_element_type=F32)
+            if n > 0:
+                value = total[:, at] + value
+            if hi < SLOTS:
+                total[:, at] = value
+            else:
+                result[:, at] = value.astype(BF16)
             return 0
 
         lax.fori_loop(0, width // 512, tile, 0, unroll=hi == SLOTS)
@@ -346,7 +359,8 @@
         for k in range(4):
             for half in (0, 1):
                 first[half, k][stage]()
-    combine(0)
+    for a in (0, 1):
+        combine(0, a)
     for k in range(4):
         for half in (0, 1):
             first[half, k][2]()
@@ -354,8 +368,9 @@
         for half in (0, 1):
             second[half][stage]()
     weight_grad[...] = term[mine]
-    combine(1)
-    combine(2)
+    for n in (1, 2):
+        for a in (0, 1):
+            combine(n, a)
     for copy in sent:
         copy.wait_send()
 
@@ -364,7 +379,7 @@
     sources, targets, sems = refs[:3], refs[3:6], refs[6]
     copies = []
     for i, (src, dst) in enumerate(zip(sources, targets)):
-        parts = 4 if src.shape[0] % 4 == 0 else 3
+        parts = 2 if src.shape[0] % 2 == 0 else 1
         size = src.shape[0] // parts
         for k in range(parts):
             at = pl.ds(k * size, size)
@@ -381,7 +396,7 @@
     blocks = width // part
     vmem = pl.BlockSpec(memory_space=pltpu.VMEM)
     anywhere = pl.BlockSpec(memory_space=pl.ANY)
-    slots = pltpu.VMEM((SLOTS, CAP, width), BF16)
+    pairs = pltpu.VMEM((SLOTS, 2, CAP, width), BF16)
     sem = pltpu.SemaphoreType.DMA
     shapes = (
         jax.ShapeDtypeStruct((count, width), BF16),
@@ -397,14 +412,14 @@
             pltpu.VMEM((blocks, kinds, part, hidden), BF16),
             pltpu.VMEM((blocks, kinds, part, hidden), BF16),
             pltpu.VMEM((2, 30, kinds, part // 4, hidden), BF16),
-            *([slots] * 8),
+            *([pairs] * 4),
             *([pltpu.VMEM((ROWS, width), BF16)] * 2),
             *([pltpu.VMEM((ROWS, hidden), BF16)] * 3),
             *([pltpu.VMEM((ROWS, count), BF16)] * 2),
             *([pltpu.VMEM((count, width), BF16)] * 2),
             *([pltpu.VMEM((count, width), F32)] * 2),
             *(pltpu.VMEM((2, count, CAP * (hi - lo)), BF16) for lo, hi in CHUNKS),
-            sem((2, SLOTS)), sem((2, SLOTS)), sem((2, SLOTS)), sem((2, SLOTS)),
+            *([sem((SLOTS,))] * 4),
             sem((2, 20)), sem((2, 20)), sem((2, 30)), sem((2, 30)), sem((3,)),
         ],
         compiler_params=pltpu.CompilerParams(
@@ -417,7 +432,7 @@
         out_shape=shapes,
         in_specs=[anywhere] * 3,
         out_specs=(anywhere,) * 3,
-        scratch_shapes=[sem((3, 4))],
+        scratch_shapes=[sem((3, 2))],
         name="hand_out",
     )(*(pltpu.with_memory_space_constraint(a, pltpu.VMEM) for a in results))
     return moe_out, token_grad, jnp.transpose(weight_grad, (1, 0, 2))[None]

time: 153 us -> 154 us (level)
  Pallas kernels: 151 us -> 153 us
where the time goes in v4:
time: 154 us
  Pallas kernels  153 us (99%)
    pallas_call x1, Pallas kernels, on_device(): pl.pallas_call(kernel, out_shape=tuple((pltpu.VMEM(a.shape, a.dtype) for...  151 us

profile of v4, /device:TPU:33, one launch (start us, length us, event | category | flops | bytes accessed | tf_op | source)
XLA Modules:
  0.0 153.6 jit_solution(2819778529129840063)
XLA Ops:
  0.6 151.4 %experts.1 = (bf16[256,2048]{1,0:T(8,128)(2,1)S(1)}, bf16[256,2048]{1,0:T(8,128)(2,1)S(1)}, bf16[3,128,768]{2,1,0:T(8,128)(2,1)S(1)}) custom-call(bf16[256,2048]{1,0:T(8,128)(2,1)} %tokens_in.1, s32[8,256]{1,0:T(8,128)} %bitcast.9, s32[8,256]{1,0:T(8,128)} %bitcast.10, bf16[3,128,768]{2,1,0:T(8,128)(2,1)} %bitcast.8, bf16[256,2048]{1,0:T(8,128)(2,1)} %out_grad_in.1), custom_call_target="tpu_custom_call" | custom-call | tf_op jit(solution)/shard_map/experts/pallas_call | solution.py:406
  152.0 1.6 %hand_out.1 = (bf16[256,2048]{1,0:T(8,128)(2,1)}, bf16[256,2048]{1,0:T(8,128)(2,1)}, bf16[3,128,768]{2,1,0:T(8,128)(2,1)}) custom-call(bf16[256,2048]{1,0:T(8,128)(2,1)S(1)} %get-tuple-element.9.refs_0_, bf16[256,2048]{1,0:T(8,128)(2,1)S(1)} %get-tuple-element.10.refs_1_, bf16[3,128,768]{2,1,0:T(8,128)(2,1)S(1)} %get-tuple-element.11.refs_2_), custom_call_target="tpu_custom_call" | custom-call | tf_op jit(solution)/shard_map/hand_out/pallas_call | solution.py:430

commit v5 on v4

--- a/solution.py
+++ b/solution.py
@@ -14,7 +14,7 @@
 BF16 = jnp.bfloat16
 F32 = jnp.float32
 
-STEPS = (0, 1, 7, 2, 6, 3, 5, 4)
+STEPS = (0, 7, 1, 6, 2, 5, 3, 4)
 OFFSETS = [(dz, dc) for dz in STEPS for dc in (0, 1)]
 OWN = OFFSETS.index((0, 0))
 CHUNKS = ((0, 10), (10, 14), (14, 16))

time: 154 us -> 153 us (level)
  Pallas kernels: 153 us -> 151 us
where the time goes in v5:
time: 153 us; the launch traced here: 152 us
  Pallas kernels  151 us (99%)
    pallas_call x1, Pallas kernels, on_device(): pl.pallas_call(kernel, out_shape=tuple((pltpu.VMEM(a.shape, a.dtype) for...  150 us

profile of v5, /device:TPU:33, one launch (start us, length us, event | category | flops | bytes accessed | tf_op | source)
XLA Modules:
  0.0 152.1 jit_solution(16272779431503499155)
XLA Ops:
  0.6 149.9 %experts.1 = (bf16[256,2048]{1,0:T(8,128)(2,1)S(1)}, bf16[256,2048]{1,0:T(8,128)(2,1)S(1)}, bf16[3,128,768]{2,1,0:T(8,128)(2,1)S(1)}) custom-call(bf16[256,2048]{1,0:T(8,128)(2,1)} %tokens_in.1, s32[8,256]{1,0:T(8,128)} %bitcast.9, s32[8,256]{1,0:T(8,128)} %bitcast.10, bf16[3,128,768]{2,1,0:T(8,128)(2,1)} %bitcast.8, bf16[256,2048]{1,0:T(8,128)(2,1)} %out_grad_in.1), custom_call_target="tpu_custom_call" | custom-call | tf_op jit(solution)/shard_map/experts/pallas_call | solution.py:406
  150.5 1.6 %hand_out.1 = (bf16[256,2048]{1,0:T(8,128)(2,1)}, bf16[256,2048]{1,0:T(8,128)(2,1)}, bf16[3,128,768]{2,1,0:T(8,128)(2,1)}) custom-call(bf16[256,2048]{1,0:T(8,128)(2,1)S(1)} %get-tuple-element.9.refs_0_, bf16[256,2048]{1,0:T(8,128)(2,1)S(1)} %get-tuple-element.10.refs_1_, bf16[3,128,768]{2,1,0:T(8,128)(2,1)S(1)} %get-tuple-element.11.refs_2_), custom_call_target="tpu_custom_call" | custom-call | tf_op jit(solution)/shard_map/hand_out/pallas_call | solution.py:430

commit v6 on v5

--- a/solution.py
+++ b/solution.py
@@ -14,11 +14,11 @@
 BF16 = jnp.bfloat16
 F32 = jnp.float32
 
-STEPS = (0, 7, 1, 6, 2, 5, 3, 4)
+STEPS = (0, 7, 1, 6, 2, 4, 5, 3)
 OFFSETS = [(dz, dc) for dz in STEPS for dc in (0, 1)]
 OWN = OFFSETS.index((0, 0))
-CHUNKS = ((0, 10), (10, 14), (14, 16))
-PIECES = ((2, 4), (4, 6), (6, 10), (10, 14), (14, 16), (0, 2))
+CHUNKS = ((0, 10), (10, 12), (12, 16))
+PIECES = ((2, 4), (4, 6), (6, 10), (10, 12), (12, 16), (0, 2))
 
 
 def place():

time: 153 us -> 153 us (level)
  no operation moved by 1% of the time
where the time goes in v6:
time: 153 us
  Pallas kernels  152 us (99%)
    pallas_call x1, Pallas kernels, on_device(): pl.pallas_call(kernel, out_shape=tuple((pltpu.VMEM(a.shape, a.dtype) for...  151 us

profile of v6, /device:TPU:33, one launch (start us, length us, event | category | flops | bytes accessed | tf_op | source)
XLA Modules:
  0.0 152.8 jit_solution(14816580369936132128)
XLA Ops:
  0.6 150.6 %experts.1 = (bf16[256,2048]{1,0:T(8,128)(2,1)S(1)}, bf16[256,2048]{1,0:T(8,128)(2,1)S(1)}, bf16[3,128,768]{2,1,0:T(8,128)(2,1)S(1)}) custom-call(bf16[256,2048]{1,0:T(8,128)(2,1)} %tokens_in.1, s32[8,256]{1,0:T(8,128)} %bitcast.9, s32[8,256]{1,0:T(8,128)} %bitcast.10, bf16[3,128,768]{2,1,0:T(8,128)(2,1)} %bitcast.8, bf16[256,2048]{1,0:T(8,128)(2,1)} %out_grad_in.1), custom_call_target="tpu_custom_call" | custom-call | tf_op jit(solution)/shard_map/experts/pallas_call | solution.py:406
  151.2 1.6 %hand_out.1 = (bf16[256,2048]{1,0:T(8,128)(2,1)}, bf16[256,2048]{1,0:T(8,128)(2,1)}, bf16[3,128,768]{2,1,0:T(8,128)(2,1)}) custom-call(bf16[256,2048]{1,0:T(8,128)(2,1)S(1)} %get-tuple-element.9.refs_0_, bf16[256,2048]{1,0:T(8,128)(2,1)S(1)} %get-tuple-element.10.refs_1_, bf16[3,128,768]{2,1,0:T(8,128)(2,1)S(1)} %get-tuple-element.11.refs_2_), custom_call_target="tpu_custom_call" | custom-call | tf_op jit(solution)/shard_map/hand_out/pallas_call | solution.py:430
